TPU v7x, 32 devices: a whole 2x2x4 slice. The times are simulated.
32 devices in a mesh: groups: 2 (over y), slab: 4 (over z), sub: 4 (over x, core).
Axes of the slice: x: 2, y: 2, z: 4, core: 2. Of those that a mesh axis runs over, the one named last changes fastest.
Arguments:
- blocks: bfloat16 [512, 7, 128, 128], P(('groups', 'slab', 'sub')), parts along dimension 0, may hold values from -6 to 6
- prolong: bfloat16 [512, 32, 128], P(('groups', 'slab', 'sub')), parts along dimension 0, may hold values from -0.5 to 0.5
- columns: int32 [512, 7], P(('groups', 'slab', 'sub')), parts along dimension 0, may hold values from 0 to 255, as said below
- live: int32 [512, 7], P(('groups', 'slab', 'sub')), parts along dimension 0, may hold values from 0 to 1, as said below
- slots: int32 [512, 7], P(('groups', 'slab', 'sub')), parts along dimension 0, may hold values from 0 to 7
- coarse_of: int32 [512], P(('groups', 'slab', 'sub')), parts along dimension 0, may hold values from 0 to 63, as said below
Outputs:
- coarse: float32 [128, 32, 256], P(('groups', 'slab', 'sub')), parts along dimension 0
There are 2 independent parts, one for each index of `groups`. A program takes and returns all parts, laid end to end along the dimension named above; each array names one. Nothing has to cross between parts.
Inputs may be any that keep to these rules, and one draw needn't show every extreme that they name: columns[i, 0] = i; every column lies in the slab of block rows [s * 64, (s + 1) * 64) that holds i, or in one of the two slabs beside it. live[i, 0] = 1. coarse_of[i] lies in the coarse slab [s * 16, (s + 1) * 16) that holds i // 4, or in one of the two coarse slabs beside it.
All inputs are finite; a program needn't handle non-finite values.
Results may differ from a plain program's by a relative error of at most 0.0029.
Values may be sent and summed in bfloat16 or wider, within the bound.
A program may use at most 128 MiB of HBM per device.

v0:
```python
import jax
import jax.numpy as jnp
from jax import lax
from jax.sharding import PartitionSpec as P

BS = 128
CB = 32
KC = 8


def padded_2(block, sides, width):
    for axis, dim in sides:
        count = lax.axis_size(axis)
        forward = [(i, i + 1) for i in range(count - 1)]
        backward = [(target, source) for source, target in forward]
        low = lax.ppermute(
            lax.slice_in_dim(block, block.shape[dim] - width, None, axis=dim), axis, forward
        )
        high = lax.ppermute(lax.slice_in_dim(block, 0, width, axis=dim), axis, backward)
        block = jnp.concatenate([low, block, high], axis=dim)
    return block


def body(blocks, prolong, columns, live, slots, coarse_of):
    rows = prolong.shape[0]
    neighbours = blocks.shape[1]
    n_sub = lax.axis_size("sub")
    slab_rows = rows * n_sub
    slab_coarse = slab_rows // 4
    slab_pos = lax.axis_index("slab")
    slab_prolong = lax.all_gather(prolong, "sub", axis=0, tiled=True)
    widened = padded_2(slab_prolong, (("slab", 0),), slab_rows)
    first_row = (slab_pos - 1) * slab_rows
    local_cols = (columns - first_row).reshape(-1)
    far_rows = jnp.take(widened, local_cols, axis=0)
    flat_blocks = blocks.reshape(rows * neighbours, BS, BS)
    applied = jnp.einsum("ecb,eab->eca", far_rows, flat_blocks, preferred_element_type=jnp.float32)
    applied = applied.astype(jnp.bfloat16).reshape(rows, neighbours, CB, BS)
    term = jnp.einsum("rxa,rkca->rkxc", prolong, applied, preferred_element_type=jnp.float32)
    term = term * live[:, :, None, None].astype(jnp.float32)
    first_coarse = (slab_pos - 1) * slab_coarse
    target = ((coarse_of[:, None] - first_coarse) * KC + slots).reshape(-1)
    window = jax.ops.segment_sum(
        term.reshape(rows * neighbours, CB, CB), target, num_segments=3 * slab_coarse * KC
    )
    window = (
        window.reshape(3, slab_coarse, KC, CB, CB)
        .transpose(0, 1, 3, 2, 4)
        .reshape(3, slab_coarse, CB, KC * CB)
    )
    padded = padded_2(window, (("slab", 0),), 1)
    own_slab = padded[2] + padded[0] + padded[4]
    return lax.psum_scatter(own_slab, "sub", scatter_dimension=0, tiled=True)


def solution(mesh):
    in_specs = (
        P(("groups", "slab", "sub"), None, None, None),
        P(("groups", "slab", "sub"), None, None),
        P(("groups", "slab", "sub"), None),
        P(("groups", "slab", "sub"), None),
        P(("groups", "slab", "sub"), None),
        P(("groups", "slab", "sub")),
    )
    out_specs = P(("groups", "slab", "sub"), None, None)
    return jax.shard_map(body, mesh=mesh, in_specs=in_specs, out_specs=out_specs, check_vma=False)
```

profile of v0, /device:TPU:0, one launch (start us, length us, event | category | flops | bytes accessed | tf_op | source)
XLA Modules:
  0.0 121.2 jit_solution(17727559069059963122)
XLA Ops:
  6.5 0.0 reduce-scatter.2.cloned.1.call-start
  6.5 8.8 %all_gather.3 = bf16[64,32,128]{2,1,0:T(8,128)(2,1)S(1)} all-gather(bf16[16,32,128]{2,1,0:T(8,128)(2,1)} %param.7), channel_id=1, replica_groups=mesh['groups'=2,'slab'=4,'sub'=4] {'sub'}, dimensions={0}, use_global_device_ids=true | all-gather | bytes 655360 | tf_op jit(solution)/shard_map/all_gather | solution.py:31
  15.4 1.3 %collective-permute-start.1 = (bf16[64,32,128]{2,1,0:T(8,128)(2,1)S(1)}, bf16[64,32,128]{2,1,0:T(8,128)(2,1)S(1)}, u32[]{:S(2)}, u32[]{:S(2)}) collective-permute-start(bf16[64,32,128]{2,1,0:T(8,128)(2,1)S(1)} %all_gather.3), channel_id=1, source_target_pairs={{4,0},{8,4},{12,8},{5,1},{9,5},{13,9},{6,2},{10,6},{14,10},{7,3},{... | collective-permute-start | bytes 1572872 | tf_op jit(solution)/shard_map/ppermute | solution.py:19
  16.6 4.6 %collective-permute-start = (bf16[64,32,128]{2,1,0:T(8,128)(2,1)S(1)}, bf16[64,32,128]{2,1,0:T(8,128)(2,1)S(1)}, u32[]{:S(2)}, u32[]{:S(2)}) collective-permute-start(bf16[64,32,128]{2,1,0:T(8,128)(2,1)S(1)} %all_gather.3), channel_id=1, source_target_pairs={{0,4},{4,8},{8,12},{1,5},{5,9},{9,13},{2,6},{6,10},{10,14},{3,7},{... | collective-permute-start | bytes 1572872 | tf_op jit(solution)/shard_map/ppermute | solution.py:16
  21.2 0.7 broadcast_subtract_fusion
  21.9 0.1 copy.25
  22.0 0.1 reshape.62
  22.1 0.1 reshape.61
  22.2 0.7 subtract_multiply_fusion
  22.9 0.7 broadcast_add_fusion
  23.5 0.1 copy.24
  23.6 0.1 reshape.77
  23.7 0.7 convert_element_type.8
  24.4 0.1 copy.27
  24.5 6.9 %collective-permute-done.1 = bf16[64,32,128]{2,1,0:T(8,128)(2,1)S(1)} collective-permute-done((bf16[64,32,128]{2,1,0:T(8,128)(2,1)S(1)}, bf16[64,32,128]{2,1,0:T(8,128)(2,1)S(1)}, u32[]{:S(2)}, u32[]{:S(2)}) %collective-permute-start.1) | collective-permute-done | bytes 524320 | tf_op jit(solution)/shard_map/ppermute | solution.py:19
  31.4 1.2 collective-permute-done
  32.6 0.2 pad_maximum_fusion
  32.8 0.7 gather_fusion
  33.5 0.0 copy-start
  33.5 4.1 %convolution_convert_fusion = bf16[112,32,128]{2,1,0:T(8,128)(2,1)S(1)} fusion(bf16[112,128,128]{2,1,0:T(8,128)(2,1)} %bitcast.31, bf16[112,32,128]{2,1,0:T(8,128)(2,1)S(1)} %gather_fusion, pred[112]{0:T(512)(128)(4,1)S(1)} %compare_and_fusion), kind=kOutput, calls=%fused_computation.4 | convolution fusion | flops 118358016 | bytes 5505136 | tf_op jit(solution)/shard_map/ecb,eab->eca/dot_general | solution.py:37
  37.6 0.0 copy-done
  37.7 1.7 %convolution_multiply_fusion = f32[16,7,32,32]{3,2,1,0:T(8,128)} fusion(bf16[16,7,32,128]{3,2,1,0:T(8,128)(2,1)S(1)} %bitcast.32, f32[16,7]{1,0:T(8,128)S(1)} %copy.27, bf16[16,32,128]{2,1,0:T(8,128)(2,1)S(1)} %copy-done), kind=kOutput, calls=%fused_computation.3 | convolution fusion | flops 29474816 | bytes 1507776 | tf_op jit(solution)/shard_map/rxa,rkca->rkxc/dot_general | solution.py:39
  39.3 1.8 %copy.28 = f32[112,32,32]{2,1,0:T(8,128)S(1)} copy(f32[112,32,32]{1,2,0:T(8,128)} %bitcast.30) | data formatting | bytes 917504 | tf_op jit(solution)/shard_map/reshape | solution.py:44
  41.1 3.4 %broadcast_in_dim.15 = f32[384,32,32]{2,1,0:T(8,128)} broadcast(f32[]{:T(128)} %constant.11.clone.1), dimensions={} | broadcast | bytes 1572868 | tf_op jit(solution)/shard_map/broadcast_in_dim | solution.py:43
  44.6 13.8 %scatter_fusion = f32[384,32,32]{2,1,0:T(8,128)} fusion(f32[384,32,32]{2,1,0:T(8,128)} %broadcast_in_dim.15, s32[112]{0:T(128)S(1)} %reshape.77, f32[112,32,32]{2,1,0:T(8,128)S(1)} %copy.28), kind=kCustom, calls=%fused_computation.1 | custom fusion | flops 114688 | bytes 1376704 | tf_op jit(solution)/shard_map/scatter-add | solution.py:43
  58.4 5.9 %fusion.6 = (f32[1,16,32,8,32]{4,2,3,1,0:T(8,128)S(1)}, f32[1,16,32,8,32]{4,2,3,1,0:T(8,128)}, f32[1,16,32,8,32]{4,2,3,1,0:T(8,128)}) fusion(f32[3,16,32,8,32]{4,2,3,1,0:T(8,128)} %bitcast.29), kind=kLoop, calls=%fused_computation.20 | loop fusion | bytes 3145728 | tf_op jit(solution)/shard_map/slice | solution.py:17
  64.2 1.6 %copy.30 = f32[1,16,32,8,32]{4,3,2,1,0:T(8,128)S(1)} copy(f32[1,16,32,8,32]{4,2,3,1,0:T(8,128)S(1)} %get-tuple-element.5) | data formatting | bytes 1048576 | tf_op jit(solution)/shard_map/slice | solution.py:17
  65.9 0.6 slice.18
  66.5 5.2 %collective-permute-start.2 = (f32[1,16,32,256]{3,2,1,0:T(8,128)S(1)}, f32[1,16,32,256]{3,2,1,0:T(8,128)}, u32[]{:S(2)}, u32[]{:S(2)}) collective-permute-start(f32[1,16,32,256]{3,2,1,0:T(8,128)S(1)} %slice.18), channel_id=1, source_target_pairs={{0,4},{4,8},{8,12},{1,5},{5,9},{9,13},{2,6},{6,10},{10,14},{3,7},{... | collective-permute-start | bytes 1572872 | tf_op jit(solution)/shard_map/ppermute | solution.py:16
  71.7 3.2 %copy.31 = f32[1,16,32,8,32]{4,3,2,1,0:T(8,128)S(1)} copy(f32[1,16,32,8,32]{4,2,3,1,0:T(8,128)} %get-tuple-element.6) | data formatting | bytes 1048576 | tf_op jit(solution)/shard_map/slice | solution.py:19
  74.9 1.4 %slice.20 = f32[1,16,32,256]{3,2,1,0:T(8,128)} reshape(f32[1,16,32,8,32]{4,3,2,1,0:T(8,128)S(1)} %copy.31) | data formatting | bytes 1048576 | tf_op jit(solution)/shard_map/slice | solution.py:19
  76.3 1.5 %collective-permute-start.3 = (f32[1,16,32,256]{3,2,1,0:T(8,128)}, f32[1,16,32,256]{3,2,1,0:T(8,128)}, u32[]{:S(2)}, u32[]{:S(2)}) collective-permute-start(f32[1,16,32,256]{3,2,1,0:T(8,128)} %slice.20), channel_id=1, source_target_pairs={{4,0},{8,4},{12,8},{5,1},{9,5},{13,9},{6,2},{10,6},{14,10},{7,3},{... | collective-permute-start | bytes 1572872 | tf_op jit(solution)/shard_map/ppermute | solution.py:19
  77.8 3.2 %copy.29 = f32[1,16,32,8,32]{4,3,2,1,0:T(8,128)S(1)} copy(f32[1,16,32,8,32]{4,2,3,1,0:T(8,128)} %get-tuple-element.7) | data formatting | bytes 1048576 | tf_op jit(solution)/shard_map/slice | solution.py:52
  81.0 0.6 squeeze.9
  81.6 0.0 collective-permute-done.2
  81.6 9.5 %collective-permute-done.3 = f32[1,16,32,256]{3,2,1,0:T(8,128)} collective-permute-done((f32[1,16,32,256]{3,2,1,0:T(8,128)}, f32[1,16,32,256]{3,2,1,0:T(8,128)}, u32[]{:S(2)}, u32[]{:S(2)}) %collective-permute-start.3) | collective-permute-done | bytes 524320 | tf_op jit(solution)/shard_map/ppermute | solution.py:19
  91.1 2.1 %bitcast_add_fusion = f32[16,32,256]{2,1,0:T(8,128)} fusion(f32[1,16,32,256]{3,2,1,0:T(8,128)} %collective-permute-done.3, f32[16,32,256]{2,1,0:T(8,128)S(1)} %squeeze.9, f32[1,16,32,256]{3,2,1,0:T(8,128)} %collective-permute-done.2), kind=kLoop, calls=%fused_computation.7 | loop fusion | flops 262144 | bytes 2097152 | tf_op jit(solution)/shard_map/add | solution.py:52
  93.2 0.0 reduce-scatter.2.cloned.1.call-update
  93.2 21.1 %reduce-scatter.2.cloned.1.call-done = f32[4,32,256]{2,1,0:T(8,128)} async-done(((f32[16,32,256]{2,1,0:T(8,128)}), f32[4,32,256]{2,1,0:T(8,128)}) %reduce-scatter.2.cloned.1.call-update) | async-done | bytes 131088 | tf_op jit(solution)/shard_map/reduce_scatter | solution.py:53
  (3 shorter events, 0.0 us)
Async XLA Ops:
  6.5 107.8 %reduce-scatter.2.cloned.1.call-start = ((), (), s32[]{:S(2)}) async-start(), calls=%async_computation.1 | async-start | bytes 655360 | tf_op jit(solution)/shard_map/reduce_scatter | solution.py:53
  15.4 16.1 %collective-permute-start.1 = (bf16[64,32,128]{2,1,0:T(8,128)(2,1)S(1)}, bf16[64,32,128]{2,1,0:T(8,128)(2,1)S(1)}, u32[]{:S(2)}, u32[]{:S(2)}) collective-permute-start(bf16[64,32,128]{2,1,0:T(8,128)(2,1)S(1)} %all_gather.3), channel_id=1, source_target_pairs={{4,0},{8,4},{12,8},{5,1},{9,5},{13,9},{6,2},{10,6},{14,10},{7,3},{... | collective-permute-start | bytes 1572872 | tf_op jit(solution)/shard_map/ppermute | solution.py:19
  16.6 16.0 %collective-permute-start = (bf16[64,32,128]{2,1,0:T(8,128)(2,1)S(1)}, bf16[64,32,128]{2,1,0:T(8,128)(2,1)S(1)}, u32[]{:S(2)}, u32[]{:S(2)}) collective-permute-start(bf16[64,32,128]{2,1,0:T(8,128)(2,1)S(1)} %all_gather.3), channel_id=1, source_target_pairs={{0,4},{4,8},{8,12},{1,5},{5,9},{9,13},{2,6},{6,10},{10,14},{3,7},{... | collective-permute-start | bytes 1572872 | tf_op jit(solution)/shard_map/ppermute | solution.py:16
  33.5 4.1 %copy-start = (bf16[16,32,128]{2,1,0:T(8,128)(2,1)S(1)}, bf16[16,32,128]{2,1,0:T(8,128)(2,1)}, u32[]{:S(2)}) copy-start(bf16[16,32,128]{2,1,0:T(8,128)(2,1)} %param.7) | copy-start | bytes 393220
  66.5 15.2 %collective-permute-start.2 = (f32[1,16,32,256]{3,2,1,0:T(8,128)S(1)}, f32[1,16,32,256]{3,2,1,0:T(8,128)}, u32[]{:S(2)}, u32[]{:S(2)}) collective-permute-start(f32[1,16,32,256]{3,2,1,0:T(8,128)S(1)} %slice.18), channel_id=1, source_target_pairs={{0,4},{4,8},{8,12},{1,5},{5,9},{9,13},{2,6},{6,10},{10,14},{3,7},{... | collective-permute-start | bytes 1572872 | tf_op jit(solution)/shard_map/ppermute | solution.py:16
  76.3 14.8 %collective-permute-start.3 = (f32[1,16,32,256]{3,2,1,0:T(8,128)}, f32[1,16,32,256]{3,2,1,0:T(8,128)}, u32[]{:S(2)}, u32[]{:S(2)}) collective-permute-start(f32[1,16,32,256]{3,2,1,0:T(8,128)} %slice.20), channel_id=1, source_target_pairs={{4,0},{8,4},{12,8},{5,1},{9,5},{13,9},{6,2},{10,6},{14,10},{7,3},{... | collective-permute-start | bytes 1572872 | tf_op jit(solution)/shard_map/ppermute | solution.py:19
Sparse Core Ops, SparseCore 0:
  93.4 20.9 reduce-scatter.1
where the time goes:
time: 122 us; the launch traced here: 121 us
  waiting for transfers between devices  38.6 us (32%)
  local copies, waits for them, and re-layouts  23.1 us (19%)
  other arithmetic  18.8 us (15%)
  between operations  13.5 us (11%)
  starting transfers between devices  12.6 us (10%)
  blocking collectives  8.82 us (7%)
  matrix products  5.77 us (5%)
    reduce_scatter x1, waiting for transfers between devices, body(): return lax.psum_scatter(own_slab, 'sub', scatter_dimension=0, tiled=True)  21.1 us
    ppermute x2, waiting for transfers between devices, padded_2(): lax.ppermute(lax.slice_in_dim(block, 0, width, axis=dim), axis, backward)  16.3 us
    scatter-add x1, other arithmetic, body(): jax.ops.segment_sum(term.reshape(rows * neighbours, CB, CB), target, num_...  13.8 us
    ppermute x2, starting transfers between devices, padded_2(): lax.ppermute(lax.slice_in_dim(block, block.shape[dim] - width, None, axis...  9.82 us
    all_gather x1, blocking collectives, body(): slab_prolong = lax.all_gather(prolong, 'sub', axis=0, tiled=True)  8.82 us
    slice x3, local copies, waits for them, and re-layouts, padded_2(): lax.slice_in_dim(block, block.shape[dim] - width, None, axis=dim)  8.09 us
    slice x2, local copies, waits for them, and re-layouts, padded_2(): lax.slice_in_dim(block, 0, width, axis=dim)  4.63 us
    dot_general x1, matrix products, body(): jnp.einsum('ecb,eab->eca', far_rows, flat_blocks, preferred_element_type=...  4.12 us
  transfers between devices with their start and end apart: 5, of which 4 were waited for; matrix products, arithmetic and copies ran while one was open for 10% of the time, Pallas kernels for 0%

commit v1 on v0

v1 whole, which is shorter than its diff:
```python
import functools

import jax
import jax.numpy as jnp
from jax import lax
from jax.experimental import pallas as pl
from jax.experimental.pallas import tpu as pltpu
from jax.sharding import PartitionSpec as P

BS = 128
CB = 32
KC = 8
CORES = 2
CHUNKS = 4
MESH = pl.DeviceIdType.MESH
NT = (((1,), (1,)), ((), ()))


def kernel(n_slab, n_sub, columns, live, slots, coarse_of, prolong, blocks, out,
           wide, blk, qs, tb, dmat, wm, mrecv, wo, sb, rbuf,
           own_sem, blk_sem, p1s, p1r, fs, fr, ms, mr, p2s, p2r):
    rows, nbr = blk.shape[0], blk.shape[1]
    n_x = n_sub // CORES
    ncr = rows // 4
    piece = ncr * CB
    slab_rows = rows * n_sub
    slab_coarse = ncr * n_sub
    z = lax.axis_index("slab")
    sub = lax.axis_index("sub")
    x, c = lax.div(sub, CORES), lax.rem(sub, CORES)
    mate = sub + 1 - 2 * c
    per = rows // CHUNKS

    def there(dz, fn):
        if dz == 0:
            fn()
        else:
            pl.when(jnp.logical_and(z + dz >= 0, z + dz < n_slab))(fn)

    def place(group, owner):
        return pl.ds((group * n_sub + owner) * rows, rows)

    own = pltpu.make_async_copy(prolong, wide.at[place(1, sub)], own_sem)
    own.start()
    loads = [
        pltpu.make_async_copy(blocks.at[pl.ds(n * per, per)], blk.at[pl.ds(n * per, per)], blk_sem.at[n])
        for n in range(CHUNKS)
    ]
    for load in loads:
        load.start()

    barrier = pltpu.get_barrier_semaphore()
    offsets = [(dz, ox) for dz in (0, -1, 1) for ox in range(n_x)]
    plane = [o for o in offsets if o != (0, 0)]

    def to_sub(ox):
        return lax.rem(x + ox, n_x) * CORES + c

    def from_sub(ox, core):
        return lax.rem(x + n_x - ox, n_x) * CORES + core

    def greet(dz, ox):
        def go():
            pl.semaphore_signal(barrier, inc=1, device_id={"slab": z + dz, "sub": to_sub(ox)},
                                device_id_type=MESH)
        return go

    pl.semaphore_signal(barrier, inc=1, device_id={"sub": mate}, device_id_type=MESH)
    for dz, ox in plane:
        there(dz, greet(dz, ox))
    ends = (z == 0).astype(jnp.int32) + (z == n_slab - 1).astype(jnp.int32)
    pl.semaphore_wait(barrier, 3 * n_x - n_x * ends)

    def p1_send(dz, ox):
        return pltpu.make_async_remote_copy(
            src_ref=prolong, dst_ref=wide.at[place(1 - dz, sub)],
            send_sem=p1s.at[dz + 1, ox], recv_sem=p1r.at[dz + 1, ox],
            device_id={"slab": z + dz, "sub": to_sub(ox)}, device_id_type=MESH)

    def p1_recv(dz, ox):
        spot = wide.at[place(1 - dz, from_sub(ox, c))]
        return pltpu.make_async_remote_copy(
            src_ref=spot, dst_ref=spot,
            send_sem=p1s.at[dz + 1, ox], recv_sem=p1r.at[dz + 1, ox],
            device_id={"slab": z, "sub": mate}, device_id_type=MESH)

    def fwd(dz, ox, core):
        spot = wide.at[place(1 - dz, from_sub(ox, core))]
        return pltpu.make_async_remote_copy(
            src_ref=prolong if (dz, ox) == (0, 0) else spot, dst_ref=spot,
            send_sem=fs.at[dz + 1, ox], recv_sem=fr.at[dz + 1, ox],
            device_id={"slab": z, "sub": mate}, device_id_type=MESH)

    for dz, ox in reversed(plane):
        there(dz, lambda dz=dz, ox=ox: p1_send(dz, ox).start())
    fwd(0, 0, c).start()

    for dz in (-1, 1):
        @pl.when(jnp.logical_not(jnp.logical_and(z - dz >= 0, z - dz < n_slab)))
        def _():
            rbuf[dz + 1] = jnp.zeros(rbuf.shape[1:], rbuf.dtype)

    shape = dmat.shape
    lane = lax.broadcasted_iota(jnp.int32, shape, 1)
    row = lax.broadcasted_iota(jnp.int32, shape, 0)
    first_coarse = (z - 1) * slab_coarse
    lane_row = lax.broadcasted_iota(jnp.int32, (1, shape[1]), 1) // CB
    ce = jnp.zeros((1, shape[1]), jnp.int32)
    for i in range(rows):
        ce = jnp.where(lane_row == i, coarse_of[i] - first_coarse, ce)
    shift = (row // piece) * (CORES * ncr) + (row % piece) // CB
    dmat[...] = jnp.where(lane % CB == row % CB, ce - shift, -(2 ** 20))

    own.wait()

    def left(i):
        mine = wide[(n_sub + sub) * rows + i]
        for k in range(nbr):
            q = jnp.dot(mine, blk[i, k], preferred_element_type=jnp.float32)
            high = q.astype(jnp.bfloat16)
            low = (q - high.astype(jnp.float32)).astype(jnp.bfloat16)
            qs[i, :CB, k * BS:(k + 1) * BS] = high
            qs[i, CB:, k * BS:(k + 1) * BS] = low

    def pass_on(dz, ox):
        def go():
            p1_recv(dz, ox).wait_recv()
            fwd(dz, ox, c).start()
        there(-dz, go)

    turns = sorted(plane, key=lambda o: (o[1] > 0 and o[0] != 0, o[1]))
    for n in range(CHUNKS):
        loads[n].wait()

        @pl.loop(0, per, unroll=per)
        def _(t):
            left(n * per + t)
        if n == CHUNKS - 2:
            for o in turns[:len(turns) // 2]:
                pass_on(*o)
    for o in turns[len(turns) // 2:]:
        pass_on(*o)
    for dz, ox in offsets:
        there(-dz, lambda dz=dz, ox=ox: fwd(dz, ox, 1 - c).wait_recv())

    first_row = (z - 1) * slab_rows

    def right(i):
        parts = []
        for k in range(nbr):
            far = wide[jnp.clip(columns[k, i] - first_row, 0, 3 * slab_rows - 1)]
            slot, alive = slots[k, i], live[k, i]
            marks = [jnp.where(slot == s, alive, 0).astype(jnp.float32).astype(jnp.bfloat16) for s in range(KC)]
            parts.append(jnp.concatenate([far * m for m in marks], axis=0))
        both = lax.dot_general(qs[i], jnp.concatenate(parts, axis=1), NT,
                               preferred_element_type=jnp.float32)
        tb[pl.ds(pl.multiple_of(i * CB, CB), CB), :] = (both[:CB] + both[CB:]).astype(jnp.bfloat16)

    @pl.loop(0, rows, unroll=4)
    def _(i):
        right(i)

    def window(group, core):
        pick = (dmat[...] == group * slab_coarse + core * ncr)
        pick = jnp.where(pick, 1.0, 0.0).astype(jnp.bfloat16)
        return jnp.dot(pick, tb[...], preferred_element_type=jnp.float32)

    def over(group):
        return pltpu.make_async_remote_copy(
            src_ref=wm.at[group], dst_ref=mrecv.at[group],
            send_sem=ms.at[group], recv_sem=mr.at[group],
            device_id={"slab": z, "sub": mate}, device_id_type=MESH)

    order = (0, 2, 1)
    for g in order:
        wm[g] = window(g, 1 - c).astype(jnp.bfloat16)
        over(g).start()
    for g in order:
        wo[g] = window(g, c)

    def p2(dz, ox):
        at = pl.ds(pl.multiple_of(lax.rem(x + ox, n_x) * piece, piece), piece)
        return pltpu.make_async_remote_copy(
            src_ref=sb.at[dz + 1, at], dst_ref=rbuf.at[dz + 1, ox],
            send_sem=p2s.at[dz + 1, ox], recv_sem=p2r.at[dz + 1, ox],
            device_id={"slab": z + dz, "sub": to_sub(ox)}, device_id_type=MESH)

    for g in order:
        over(g).wait_recv()
        total = wo[g] + mrecv[g].astype(jnp.float32)
        sb[g] = total.astype(jnp.bfloat16)
        if g == 1:
            wo[g] = total
        for ox in reversed(range(n_x)):
            if (g - 1, ox) != (0, 0):
                there(g - 1, lambda dz=g - 1, ox=ox: p2(dz, ox).start())

    for dz, ox in plane:
        there(-dz, lambda dz=dz, ox=ox: p2(dz, ox).wait_recv())
    total = wo[1, pl.ds(pl.multiple_of(x * piece, piece), piece), :]
    for dz, ox in plane:
        total = total + rbuf[dz + 1, ox].astype(jnp.float32)
    out[...] = total.reshape(out.shape)

    for g in order:
        over(g).wait_send()
    for dz, ox in plane:
        there(dz, lambda dz=dz, ox=ox: p1_send(dz, ox).wait_send())
        there(dz, lambda dz=dz, ox=ox: p2(dz, ox).wait_send())
    for dz, ox in offsets:
        there(-dz, lambda dz=dz, ox=ox: fwd(dz, ox, c).wait_send())


def body(n_slab, n_sub, blocks, prolong, columns, live, slots, coarse_of):
    rows, nbr = blocks.shape[:2]
    ncr = rows // 4
    n_x = n_sub // CORES
    half = n_x * ncr * CB
    smem = pl.BlockSpec(memory_space=pltpu.SMEM)
    hbm = pl.BlockSpec(memory_space=pltpu.HBM)
    dma = pltpu.SemaphoreType.DMA
    flops = 2 * rows * nbr * CB * BS * (BS + CB)
    return pl.pallas_call(
        functools.partial(kernel, n_slab, n_sub),
        out_shape=jax.ShapeDtypeStruct((ncr, CB, KC * CB), jnp.float32),
        in_specs=[smem] * 4 + [hbm] * 2,
        out_specs=pl.BlockSpec(memory_space=pltpu.VMEM),
        scratch_shapes=[
            pltpu.VMEM((3 * n_sub * rows, CB, BS), jnp.bfloat16),
            pltpu.VMEM((rows, nbr, BS, BS), jnp.bfloat16),
            pltpu.VMEM((rows, 2 * CB, nbr * BS), jnp.bfloat16),
            pltpu.VMEM((rows * CB, KC * CB), jnp.bfloat16),
            pltpu.VMEM((half, rows * CB), jnp.int32),
            pltpu.VMEM((3, half, KC * CB), jnp.bfloat16),
            pltpu.VMEM((3, half, KC * CB), jnp.bfloat16),
            pltpu.VMEM((3, half, KC * CB), jnp.float32),
            pltpu.VMEM((3, half, KC * CB), jnp.bfloat16),
            pltpu.VMEM((3, n_x, ncr * CB, KC * CB), jnp.bfloat16),
            dma(()), dma((CHUNKS,)),
            dma((3, n_x)), dma((3, n_x)), dma((3, n_x)), dma((3, n_x)),
            dma((3,)), dma((3,)), dma((3, n_x)), dma((3, n_x)),
        ],
        compiler_params=pltpu.CompilerParams(
            collective_id=0, has_side_effects=True, vmem_limit_bytes=63 * 2 ** 20),
        cost_estimate=pl.CostEstimate(flops=flops, bytes_accessed=2 * blocks.size, transcendentals=0),
    )(columns.T, live.T, slots.T, coarse_of, prolong, blocks)


def solution(mesh):
    rows = ("groups", "slab", "sub")
    in_specs = (
        P(rows, None, None, None), P(rows, None, None),
        P(rows, None), P(rows, None), P(rows, None), P(rows),
    )
    part = functools.partial(body, mesh.shape["slab"], mesh.shape["sub"])
    return jax.shard_map(part, mesh=mesh, in_specs=in_specs, out_specs=P(rows, None, None), check_vma=False)
```

time: 122 us -> 30.5 us (0.25)
  waiting for transfers between devices: 38.6 us -> 0 us
  Pallas kernels: 0 us -> 28.8 us
  local copies, waits for them, and re-layouts: 23.1 us -> 1.57 us
  other arithmetic: 18.8 us -> 0 us
  between operations: 13.5 us -> 0.01 us
  starting transfers between devices: 12.6 us -> 0 us
  blocking collectives: 8.82 us -> 0 us
  matrix products: 5.77 us -> 0 us
    pallas_call x0 -> x1, Pallas kernels: none -> 28.8 us  [body(): pl.pallas_call(functools.partial(kernel, n_slab, n_sub), out_shape=jax.Sh...]
    reduce_scatter x1 -> x0, waiting for transfers between devices: 21.1 us -> none  [body(): return lax.psum_scatter(own_slab, 'sub', scatter_dimension=0, tiled=True)]
    ppermute x4 -> x0, waiting for transfers between devices: 17.5 us -> none  [the longest x2 16.3 us: padded_2(): lax.ppermute(lax.slice_in_dim(block, 0, width, axis=dim), axis, backward)]
    slice x6 -> x0, local copies, waits for them, and re-layouts: 15.9 us -> none  [the longest x3 8.09 us: padded_2(): lax.slice_in_dim(block, block.shape[dim] - width, None, axis=dim)]
    scatter-add x1 -> x0, other arithmetic: 13.8 us -> none  [body(): jax.ops.segment_sum(term.reshape(rows * neighbours, CB, CB), target, num_...]
    ppermute x4 -> x0, starting transfers between devices: 12.6 us -> none  [the longest x2 9.82 us: padded_2(): lax.ppermute(lax.slice_in_dim(block, block.shape[dim] - width, None, axis...]
    all_gather x1 -> x0, blocking collectives: 8.82 us -> none  [body(): slab_prolong = lax.all_gather(prolong, 'sub', axis=0, tiled=True)]
    dot_general x2 -> x0, matrix products: 5.77 us -> none  [the longest x1 4.12 us: body(): jnp.einsum('ecb,eab->eca', far_rows, flat_blocks, preferred_element_type=...]
  transfers between devices with their start and end apart: 5 -> 0, of which waited for: 4 -> 0; matrix products, arithmetic and copies ran while one was open for 10% -> 0% of each run, Pallas kernels for 0% -> 0%
where the time goes in v1:
time: 30.5 us; the launch traced here: 30.4 us
  Pallas kernels  28.8 us (94%)
  local copies, waits for them, and re-layouts  1.57 us (5%)
    pallas_call x1, Pallas kernels, body(): pl.pallas_call(functools.partial(kernel, n_slab, n_sub), out_shape=jax.Sh...  28.8 us
    unnamed x1, local copies, waits for them, and re-layouts  1.57 us

profile of v1, /device:TPU:0, one launch (start us, length us, event | category | flops | bytes accessed | tf_op | source)
XLA Modules:
  0.0 30.4 jit_solution(3180959142033216341)
XLA Ops:
  0.0 28.8 %shard_map.64 = f32[4,32,256]{2,1,0:T(8,128)} custom-call(s32[7,16]{1,0:T(8,128)} %bitcast.3, s32[7,16]{1,0:T(8,128)} %bitcast.4, s32[7,16]{1,0:T(8,128)} %bitcast.5, s32[16]{0:T(128)} %coarse_of.1, bf16[16,32,128]{2,1,0:T(8,128)(2,1)} %prolong.1, bf16[16,7,128,128]{3,2,1,0:T(8,128)(2,1)} %blocks.1), custom_call_target="tpu_custom_call" | custom-call | flops 146800640 | bytes 3670016 | tf_op jit(solution)/shard_map/pallas_call | solution.py:223
  28.8 1.6 %copy.8 = f32[4,32,256]{2,1,0:T(8,128)} copy(f32[4,32,256]{2,1,0:T(8,128)} %shard_map.64) | data formatting | bytes 262144

commit v2 on v1

v2 whole, which is shorter than its diff:
```python
import functools

import jax
import jax.numpy as jnp
from jax import lax
from jax.experimental import pallas as pl
from jax.experimental.pallas import tpu as pltpu
from jax.sharding import PartitionSpec as P

BS = 128
CB = 32
KC = 8
CORES = 2
CHUNKS = 4
MESH = pl.DeviceIdType.MESH
NT = (((1,), (1,)), ((), ()))


def kernel(n_slab, n_sub, columns, live, slots, coarse_of, prolong, blocks, out,
           wide, blk, qs, tb, ce, picks, sb, rbuf,
           own_sem, blk_sem, p1s, p1r, fs, fr, cs, cr, ts, tr, p2s, p2r):
    rows, nbr = blk.shape[0], blk.shape[1]
    n_x = n_sub // CORES
    ncr = rows // 4
    piece = ncr * CB
    slab_rows = rows * n_sub
    slab_coarse = ncr * n_sub
    z = lax.axis_index("slab")
    sub = lax.axis_index("sub")
    x, c = lax.div(sub, CORES), lax.rem(sub, CORES)
    mate = sub + 1 - 2 * c
    per = rows // CHUNKS
    to_mate = {"device_id": {"slab": z, "sub": mate}, "device_id_type": MESH}

    def there(dz, fn):
        if dz == 0:
            fn()
        else:
            pl.when(jnp.logical_and(z + dz >= 0, z + dz < n_slab))(fn)

    def place(group, owner):
        return pl.ds((group * n_sub + owner) * rows, rows)

    own = pltpu.make_async_copy(prolong, wide.at[place(1, sub)], own_sem)
    own.start()
    loads = [
        pltpu.make_async_copy(blocks.at[pl.ds(n * per, per)], blk.at[pl.ds(n * per, per)], blk_sem.at[n])
        for n in range(CHUNKS)
    ]
    for load in loads:
        load.start()

    barrier = pltpu.get_barrier_semaphore()
    offsets = [(dz, ox) for dz in (0, -1, 1) for ox in range(n_x)]
    plane = [o for o in offsets if o != (0, 0)]

    def to_sub(ox):
        return lax.rem(x + ox, n_x) * CORES + c

    def from_sub(ox, core):
        return lax.rem(x + n_x - ox, n_x) * CORES + core

    def greet(dz, ox):
        def go():
            pl.semaphore_signal(barrier, inc=1, device_id={"slab": z + dz, "sub": to_sub(ox)},
                                device_id_type=MESH)
        return go

    pl.semaphore_signal(barrier, inc=1, device_id={"sub": mate}, device_id_type=MESH)
    for dz, ox in plane:
        there(dz, greet(dz, ox))
    ends = (z == 0).astype(jnp.int32) + (z == n_slab - 1).astype(jnp.int32)
    pl.semaphore_wait(barrier, 3 * n_x - n_x * ends)

    def spot(dz, ox, core):
        return wide.at[place(1 - dz, from_sub(ox, core))]

    def p1_send(dz, ox):
        straight = dz != 0
        return pltpu.make_async_remote_copy(
            src_ref=spot(0, ox, c) if straight and ox else prolong,
            dst_ref=spot(dz, ox, c) if straight else wide.at[place(1, sub)],
            send_sem=p1s.at[dz + 1, ox], recv_sem=p1r.at[dz + 1, ox],
            device_id={"slab": z + dz, "sub": sub if straight else to_sub(ox)}, device_id_type=MESH)

    def p1_recv(dz, ox):
        return pltpu.make_async_remote_copy(
            src_ref=spot(dz, ox, c), dst_ref=spot(dz, ox, c),
            send_sem=p1s.at[dz + 1, ox], recv_sem=p1r.at[dz + 1, ox], **to_mate)

    def fwd(dz, ox, core):
        return pltpu.make_async_remote_copy(
            src_ref=prolong if (dz, ox) == (0, 0) else spot(dz, ox, core), dst_ref=spot(dz, ox, core),
            send_sem=fs.at[dz + 1, ox], recv_sem=fr.at[dz + 1, ox], **to_mate)

    for ox in range(1, n_x):
        p1_send(0, ox).start()
    for dz in (-1, 1):
        there(dz, lambda dz=dz: p1_send(dz, 0).start())
    fwd(0, 0, c).start()

    lane_row = lax.broadcasted_iota(jnp.int32, ce.shape[1:], 1) // CB
    mine = jnp.zeros(ce.shape[1:], jnp.int32)
    for i in range(rows):
        mine = jnp.where(lane_row == i, coarse_of[i], mine)
    ce[0] = mine
    ce_copy = pltpu.make_async_remote_copy(
        src_ref=ce.at[0], dst_ref=ce.at[1], send_sem=cs, recv_sem=cr, **to_mate)
    ce_copy.start()

    for dz in (-1, 1):
        @pl.when(jnp.logical_not(jnp.logical_and(z - dz >= 0, z - dz < n_slab)))
        def _():
            rbuf[dz + 1] = jnp.zeros(rbuf.shape[1:], rbuf.dtype)

    own.wait()

    def left(i):
        mine = wide[(n_sub + sub) * rows + i]
        for k in range(nbr):
            q = jnp.dot(mine, blk[i, k], preferred_element_type=jnp.float32)
            high = q.astype(jnp.bfloat16)
            low = (q - high.astype(jnp.float32)).astype(jnp.bfloat16)
            qs[i, :CB, k * BS:(k + 1) * BS] = high
            qs[i, CB:, k * BS:(k + 1) * BS] = low

    def pass_on(dz, ox):
        def go():
            p1_recv(dz, ox).wait_recv()
            if dz == 0:
                for to in (-1, 1):
                    there(to, lambda to=to: p1_send(to, ox).start())
            fwd(dz, ox, c).start()
        there(-dz, go)

    def rows_left(n):
        loads[n].wait()

        @pl.loop(0, per, unroll=per)
        def _(t):
            left(n * per + t)

    for n in range(CHUNKS // 2):
        rows_left(n)
    for ox in range(1, n_x):
        pass_on(0, ox)
    for n in range(CHUNKS // 2, CHUNKS):
        rows_left(n)
    for dz in (-1, 1):
        pass_on(dz, 0)

    ce_copy.wait_recv()
    wide_ce = jnp.concatenate([jnp.broadcast_to(ce[h, :1], (CB, rows * CB)) for h in range(CORES)], axis=1)
    lane = lax.broadcasted_iota(jnp.int32, wide_ce.shape, 1)
    row = lax.broadcasted_iota(jnp.int32, wide_ce.shape, 0)
    wide_ce = jnp.where(lane % CB == row, wide_ce - (z - 1) * slab_coarse, -(2 ** 20))
    for g in range(3):
        for t in range(n_x):
            for q in range(ncr):
                pick = wide_ce == g * slab_coarse + (t * CORES + c) * ncr + q
                picks[g, t * piece + q * CB:t * piece + (q + 1) * CB, :] = (
                    jnp.where(pick, 1.0, 0.0).astype(jnp.bfloat16))

    for ox in range(1, n_x):
        for dz in (-1, 1):
            pass_on(dz, ox)
    for dz, ox in offsets:
        there(-dz, lambda dz=dz, ox=ox: fwd(dz, ox, 1 - c).wait_recv())

    first_row = (z - 1) * slab_rows
    lane_slot = lax.broadcasted_iota(jnp.int32, (CB, KC * CB), 1) // CB

    def right(i):
        total = jnp.zeros((CB, KC * CB), jnp.float32)
        for k in range(nbr):
            far = wide[jnp.clip(columns[k, i] - first_row, 0, 3 * slab_rows - 1)]
            both = lax.dot_general(qs[i, :, k * BS:(k + 1) * BS], jnp.concatenate([far] * KC, axis=0), NT,
                                   preferred_element_type=jnp.float32)
            slot = jnp.where(live[k, i] != 0, slots[k, i], -1)
            total += jnp.where(lane_slot == slot, both[:CB] + both[CB:], 0.0)
        tb[0, pl.ds(pl.multiple_of(i * CB, CB), CB), :] = total.astype(jnp.bfloat16)

    def share(n):
        at = pl.ds(n * per * CB, per * CB)
        return pltpu.make_async_remote_copy(
            src_ref=tb.at[0, at], dst_ref=tb.at[1, at], send_sem=ts.at[n], recv_sem=tr.at[n], **to_mate)

    for n in range(CHUNKS):
        @pl.loop(0, per, unroll=per)
        def _(t):
            right(n * per + t)
        share(n).start()
    for n in range(CHUNKS):
        share(n).wait_recv()

    def p2(dz, ox):
        at = pl.ds(pl.multiple_of(lax.rem(x + ox, n_x) * piece, piece), piece)
        return pltpu.make_async_remote_copy(
            src_ref=sb.at[dz + 1, at], dst_ref=rbuf.at[dz + 1, ox],
            send_sem=p2s.at[dz + 1, ox], recv_sem=p2r.at[dz + 1, ox],
            device_id={"slab": z + dz, "sub": to_sub(ox)}, device_id_type=MESH)

    terms = tb[...].reshape(CORES * rows * CB, KC * CB)
    for g in (0, 2, 1):
        sb[g] = jnp.dot(picks[g], terms, preferred_element_type=jnp.float32).astype(jnp.bfloat16)
        for ox in reversed(range(n_x)):
            if (g - 1, ox) != (0, 0):
                there(g - 1, lambda dz=g - 1, ox=ox: p2(dz, ox).start())

    total = sb[1, pl.ds(pl.multiple_of(x * piece, piece), piece), :].astype(jnp.float32)
    for dz, ox in plane:
        there(-dz, lambda dz=dz, ox=ox: p2(dz, ox).wait_recv())
    for dz, ox in plane:
        total = total + rbuf[dz + 1, ox].astype(jnp.float32)
    out[...] = total.reshape(out.shape)

    ce_copy.wait_send()
    for n in range(CHUNKS):
        share(n).wait_send()
    for dz, ox in plane:
        there(dz, lambda dz=dz, ox=ox: p1_send(dz, ox).wait_send())
        there(dz, lambda dz=dz, ox=ox: p2(dz, ox).wait_send())
    for dz, ox in offsets:
        there(-dz, lambda dz=dz, ox=ox: fwd(dz, ox, c).wait_send())


def body(n_slab, n_sub, blocks, prolong, columns, live, slots, coarse_of):
    rows, nbr = blocks.shape[:2]
    ncr = rows // 4
    n_x = n_sub // CORES
    half = n_x * ncr * CB
    smem = pl.BlockSpec(memory_space=pltpu.SMEM)
    hbm = pl.BlockSpec(memory_space=pltpu.HBM)
    dma = pltpu.SemaphoreType.DMA
    flops = 2 * rows * nbr * CB * BS * (BS + CB)
    return pl.pallas_call(
        functools.partial(kernel, n_slab, n_sub),
        out_shape=jax.ShapeDtypeStruct((ncr, CB, KC * CB), jnp.float32),
        in_specs=[smem] * 4 + [hbm] * 2,
        out_specs=pl.BlockSpec(memory_space=pltpu.VMEM),
        scratch_shapes=[
            pltpu.VMEM((3 * n_sub * rows, CB, BS), jnp.bfloat16),
            pltpu.VMEM((rows, nbr, BS, BS), jnp.bfloat16),
            pltpu.VMEM((rows, 2 * CB, nbr * BS), jnp.bfloat16),
            pltpu.VMEM((CORES, rows * CB, KC * CB), jnp.bfloat16),
            pltpu.VMEM((CORES, 8, rows * CB), jnp.int32),
            pltpu.VMEM((3, half, CORES * rows * CB), jnp.bfloat16),
            pltpu.VMEM((3, half, KC * CB), jnp.bfloat16),
            pltpu.VMEM((3, n_x, ncr * CB, KC * CB), jnp.bfloat16),
            dma(()), dma((CHUNKS,)),
            dma((3, n_x)), dma((3, n_x)), dma((3, n_x)), dma((3, n_x)),
            dma(()), dma(()), dma((CHUNKS,)), dma((CHUNKS,)), dma((3, n_x)), dma((3, n_x)),
        ],
        compiler_params=pltpu.CompilerParams(
            collective_id=0, has_side_effects=True, vmem_limit_bytes=63 * 2 ** 20),
        cost_estimate=pl.CostEstimate(flops=flops, bytes_accessed=2 * blocks.size, transcendentals=0),
    )(columns.T, live.T, slots.T, coarse_of, prolong, blocks)


def solution(mesh):
    rows = ("groups", "slab", "sub")
    in_specs = (
        P(rows, None, None, None), P(rows, None, None),
        P(rows, None), P(rows, None), P(rows, None), P(rows),
    )
    part = functools.partial(body, mesh.shape["slab"], mesh.shape["sub"])
    return jax.shard_map(part, mesh=mesh, in_specs=in_specs, out_specs=P(rows, None, None), check_vma=False)
```

time: 30.5 us -> 26.9 us (0.88)
  Pallas kernels: 28.8 us -> 25.2 us
    pallas_call x1, Pallas kernels: 28.8 us -> 25.2 us  [body(): pl.pallas_call(functools.partial(kernel, n_slab, n_sub), out_shape=jax.Sh...]
where the time goes in v2:
time: 26.9 us; the launch traced here: 26.7 us
  Pallas kernels  25.2 us (94%)
  local copies, waits for them, and re-layouts  1.57 us (6%)
    pallas_call x1, Pallas kernels, body(): pl.pallas_call(functools.partial(kernel, n_slab, n_sub), out_shape=jax.Sh...  25.2 us
    unnamed x1, local copies, waits for them, and re-layouts  1.57 us

profile of v2, /device:TPU:0, one launch (start us, length us, event | category | flops | bytes accessed | tf_op | source)
XLA Modules:
  0.0 26.7 jit_solution(11373477783074310149)
XLA Ops:
  0.0 25.2 %shard_map.64 = f32[4,32,256]{2,1,0:T(8,128)} custom-call(s32[7,16]{1,0:T(8,128)} %bitcast.3, s32[7,16]{1,0:T(8,128)} %bitcast.4, s32[7,16]{1,0:T(8,128)} %bitcast.5, s32[16]{0:T(128)} %coarse_of.1, bf16[16,32,128]{2,1,0:T(8,128)(2,1)} %prolong.1, bf16[16,7,128,128]{3,2,1,0:T(8,128)(2,1)} %blocks.1), custom_call_target="tpu_custom_call" | custom-call | flops 146800640 | bytes 3670016 | tf_op jit(solution)/shard_map/pallas_call | solution.py:236
  25.2 1.6 %copy.8 = f32[4,32,256]{2,1,0:T(8,128)} copy(f32[4,32,256]{2,1,0:T(8,128)} %shard_map.64) | data formatting | bytes 262144

commit v3 on v2

v3 whole, which is shorter than its diff:
```python
import functools

import jax
import jax.numpy as jnp
from jax import lax
from jax.experimental import pallas as pl
from jax.experimental.pallas import tpu as pltpu
from jax.sharding import PartitionSpec as P

BS = 128
CB = 32
KC = 8
CORES = 2
CHUNKS = 4
HALVES = 2
DIRECT = 0
SHARES = 1
MESH = pl.DeviceIdType.MESH
NT = (((1,), (1,)), ((), ()))


def kernel(n_slab, n_sub, columns_in, live_in, slots_in, coarse_of_in, prolong, blocks, out,
           columns, live, slots, coarse_of, wide, blk, qs, sel, th, tb, ce, picks, wo, sb, rbuf,
           int_sem, own_sem, blk_sem, p1s, p1r, fs, fr, cs, cr, ts, tr, p2s, p2r):
    rows, nbr = blk.shape[0], blk.shape[1]
    n_x = n_sub // CORES
    ncr = rows // 4
    piece = ncr * CB
    slab_rows = rows * n_sub
    slab_coarse = ncr * n_sub
    z = lax.axis_index("slab")
    sub = lax.axis_index("sub")
    x, c = lax.div(sub, CORES), lax.rem(sub, CORES)
    mate = sub + 1 - 2 * c
    per = rows // CHUNKS
    to_mate = {"device_id": {"slab": z, "sub": mate}, "device_id_type": MESH}

    def there(dz, fn):
        if dz == 0:
            fn()
        else:
            pl.when(jnp.logical_and(z + dz >= 0, z + dz < n_slab))(fn)

    part = rows // HALVES

    def place(group, owner, h=None):
        first = (group * n_sub + owner) * rows
        return pl.ds(first, rows) if h is None else pl.ds(first + h * part, part)

    own = pltpu.make_async_copy(prolong, wide.at[place(1, sub)], own_sem)
    own.start()
    loads = [
        pltpu.make_async_copy(blocks.at[pl.ds(n * per, per)], blk.at[pl.ds(n * per, per)], blk_sem.at[n])
        for n in range(CHUNKS)
    ]
    for load in loads:
        load.start()
    ints = [
        pltpu.make_async_copy(given, kept, int_sem.at[n])
        for n, (given, kept) in enumerate(((coarse_of_in, coarse_of), (slots_in, slots), (live_in, live),
                                           (columns_in, columns)))
    ]
    for copy in ints:
        copy.start()

    barrier = pltpu.get_barrier_semaphore()
    offsets = [(dz, ox) for dz in (0, -1, 1) for ox in range(n_x)]
    plane = [o for o in offsets if o != (0, 0)]

    def to_sub(ox):
        return lax.rem(x + ox, n_x) * CORES + c

    def from_sub(ox, core):
        return lax.rem(x + n_x - ox, n_x) * CORES + core

    def greet(dz, ox):
        def go():
            pl.semaphore_signal(barrier, inc=1, device_id={"slab": z + dz, "sub": to_sub(ox)},
                                device_id_type=MESH)
        return go

    pl.semaphore_signal(barrier, inc=1, device_id={"sub": mate}, device_id_type=MESH)
    for dz, ox in plane:
        there(dz, greet(dz, ox))
    ends = (z == 0).astype(jnp.int32) + (z == n_slab - 1).astype(jnp.int32)
    pl.semaphore_wait(barrier, 3 * n_x - n_x * ends)

    def spot(dz, ox, core, h):
        return wide.at[place(1 - dz, from_sub(ox, core), h)]

    def p1_send(dz, ox, h):
        passed = dz != 0 and ox != 0 and h < HALVES - DIRECT
        return pltpu.make_async_remote_copy(
            src_ref=spot(0, ox, c, h) if passed else prolong.at[pl.ds(h * part, part)],
            dst_ref=spot(dz, ox, c, h) if passed else wide.at[place(1 - dz, sub, h)],
            send_sem=p1s.at[dz + 1, ox, h], recv_sem=p1r.at[dz + 1, ox, h],
            device_id={"slab": z + dz, "sub": sub if passed else to_sub(ox)}, device_id_type=MESH)

    def p1_recv(dz, ox, h):
        return pltpu.make_async_remote_copy(
            src_ref=spot(dz, ox, c, h), dst_ref=spot(dz, ox, c, h),
            send_sem=p1s.at[dz + 1, ox, h], recv_sem=p1r.at[dz + 1, ox, h], **to_mate)

    def fwd(dz, ox, core, h):
        return pltpu.make_async_remote_copy(
            src_ref=prolong.at[pl.ds(h * part, part)] if (dz, ox) == (0, 0) else spot(dz, ox, core, h),
            dst_ref=spot(dz, ox, core, h),
            send_sem=fs.at[dz + 1, ox, h], recv_sem=fr.at[dz + 1, ox, h], **to_mate)

    halves = range(HALVES)
    for h in halves:
        for ox in range(1, n_x):
            p1_send(0, ox, h).start()
        for dz in (-1, 1):
            there(dz, lambda dz=dz, h=h: p1_send(dz, 0, h).start())
    for h in halves[HALVES - DIRECT:]:
        for ox in range(1, n_x):
            for dz in (-1, 1):
                there(dz, lambda dz=dz, ox=ox, h=h: p1_send(dz, ox, h).start())
    for h in halves:
        fwd(0, 0, c, h).start()

    lane_row = lax.broadcasted_iota(jnp.int32, ce.shape[1:], 1) // CB
    mine = jnp.zeros(ce.shape[1:], jnp.int32)
    for copy in ints:
        copy.wait()
    for i in range(rows):
        mine = jnp.where(lane_row == i, coarse_of[i], mine)
    ce[0] = mine
    ce_copy = pltpu.make_async_remote_copy(
        src_ref=ce.at[0], dst_ref=ce.at[1], send_sem=cs, recv_sem=cr, **to_mate)
    ce_copy.start()

    for dz in (-1, 1):
        @pl.when(jnp.logical_not(jnp.logical_and(z - dz >= 0, z - dz < n_slab)))
        def _():
            rbuf[dz + 1] = jnp.zeros(rbuf.shape[1:], rbuf.dtype)

    own.wait()

    def left(i):
        mine = wide[(n_sub + sub) * rows + i]
        for k in range(nbr):
            q = jnp.dot(mine, blk[i, k], preferred_element_type=jnp.float32)
            high = q.astype(jnp.bfloat16)
            low = (q - high.astype(jnp.float32)).astype(jnp.bfloat16)
            qs[i, k * CB:(k + 1) * CB, :BS] = high
            qs[i, k * CB:(k + 1) * CB, BS:] = low

    def pass_on(dz, ox, h):
        def go():
            p1_recv(dz, ox, h).wait_recv()
            if dz == 0 and h < HALVES - DIRECT:
                for to in (-1, 1):
                    there(to, lambda to=to: p1_send(to, ox, h).start())
            fwd(dz, ox, c, h).start()
        there(-dz, go)

    def rows_left(n):
        loads[n].wait()

        @pl.loop(0, per, unroll=per)
        def _(t):
            left(n * per + t)

    for n in range(CHUNKS // 2):
        rows_left(n)
    for ox in range(1, n_x):
        pass_on(0, ox, 0)
    rows_left(CHUNKS // 2)
    for h in halves[1:]:
        for ox in range(1, n_x):
            pass_on(0, ox, h)
    for n in range(CHUNKS // 2 + 1, CHUNKS):
        rows_left(n)

    key = lax.broadcasted_iota(jnp.int32, (CB, KC * CB), 1)
    key = jnp.where(key % CB == lax.broadcasted_iota(jnp.int32, key.shape, 0), key // CB, -2)

    @pl.loop(0, rows, unroll=2)
    def _(i):
        for k in range(nbr):
            slot = jnp.where(live[k, i] != 0, slots[k, i], -1)
            sel[i, k * CB:(k + 1) * CB, :] = jnp.where(key == slot, 1.0, 0.0).astype(jnp.bfloat16)

    for h in halves:
        for dz in (-1, 1):
            pass_on(dz, 0, h)

    ce_copy.wait_recv()
    wide_ce = jnp.concatenate([jnp.broadcast_to(ce[h, :1], (CB, rows * CB)) for h in range(CORES)], axis=1)
    lane = lax.broadcasted_iota(jnp.int32, wide_ce.shape, 1)
    row = lax.broadcasted_iota(jnp.int32, wide_ce.shape, 0)
    wide_ce = jnp.where(lane % CB == row, wide_ce - (z - 1) * slab_coarse, -(2 ** 20))
    for g in range(3):
        for t in range(n_x):
            for q in range(ncr):
                pick = wide_ce == g * slab_coarse + (t * CORES + c) * ncr + q
                picks[g, t * piece + q * CB:t * piece + (q + 1) * CB, :] = (
                    jnp.where(pick, 1.0, 0.0).astype(jnp.bfloat16))

    for h in reversed(halves):
        for ox in range(1, n_x):
            for dz in (-1, 1):
                pass_on(dz, ox, h)
    for h in halves:
        for dz, ox in offsets:
            there(-dz, lambda dz=dz, ox=ox, h=h: fwd(dz, ox, 1 - c, h).wait_recv())

    first_row = (z - 1) * slab_rows
    lane_term = lax.broadcasted_iota(jnp.int32, (CB, nbr * CB), 1) // CB

    def right(i):
        far = jnp.concatenate(
            [wide[jnp.clip(columns[k, i] - first_row, 0, 3 * slab_rows - 1)] for k in range(nbr)], axis=0)
        every = lax.dot_general(qs[i], jnp.concatenate([far, far], axis=1), NT,
                                preferred_element_type=jnp.float32)
        term = every[:CB]
        for k in range(1, nbr):
            term = jnp.where(lane_term == k, every[k * CB:(k + 1) * CB], term)
        high = term.astype(jnp.bfloat16)
        low = (term - high.astype(jnp.float32)).astype(jnp.bfloat16)
        th[i, :CB] = high
        th[i, CB:] = low

    def put(i):
        placed = jnp.dot(th[i], sel[i], preferred_element_type=jnp.float32)
        tb[0, pl.ds(pl.multiple_of(i * CB, CB), CB), :] = (placed[:CB] + placed[CB:]).astype(jnp.bfloat16)

    each = rows // SHARES

    def share(n):
        at = pl.ds(n * each * CB, each * CB)
        return pltpu.make_async_remote_copy(
            src_ref=tb.at[0, at], dst_ref=tb.at[1, at], send_sem=ts.at[n], recv_sem=tr.at[n], **to_mate)

    @pl.loop(0, rows, unroll=16)
    def _(i):
        right(i)

    for n in range(SHARES):
        @pl.loop(0, each, unroll=each)
        def _(t):
            put(n * each + t)
        share(n).start()

    groups = (0, 2, 1)
    for g in groups:
        wo[g] = jnp.dot(picks[g, :, :rows * CB], tb[0], preferred_element_type=jnp.float32)
    for n in range(SHARES):
        share(n).wait_recv()

    def p2(dz, ox):
        at = pl.ds(pl.multiple_of(lax.rem(x + ox, n_x) * piece, piece), piece)
        return pltpu.make_async_remote_copy(
            src_ref=sb.at[dz + 1, at], dst_ref=rbuf.at[dz + 1, ox],
            send_sem=p2s.at[dz + 1, ox], recv_sem=p2r.at[dz + 1, ox],
            device_id={"slab": z + dz, "sub": to_sub(ox)}, device_id_type=MESH)

    for g in groups:
        sb[g] = (wo[g] + jnp.dot(picks[g, :, rows * CB:], tb[1], preferred_element_type=jnp.float32)).astype(jnp.bfloat16)
        for ox in reversed(range(n_x)):
            if (g - 1, ox) != (0, 0):
                there(g - 1, lambda dz=g - 1, ox=ox: p2(dz, ox).start())

    total = sb[1, pl.ds(pl.multiple_of(x * piece, piece), piece), :].astype(jnp.float32)
    for dz, ox in plane:
        there(-dz, lambda dz=dz, ox=ox: p2(dz, ox).wait_recv())
    for dz, ox in plane:
        total = total + rbuf[dz + 1, ox].astype(jnp.float32)
    out[...] = total.reshape(out.shape)

    ce_copy.wait_send()
    for n in range(SHARES):
        share(n).wait_send()
    for dz, ox in plane:
        there(dz, lambda dz=dz, ox=ox: p2(dz, ox).wait_send())
        for h in halves:
            there(dz, lambda dz=dz, ox=ox, h=h: p1_send(dz, ox, h).wait_send())
    for dz, ox in offsets:
        for h in halves:
            there(-dz, lambda dz=dz, ox=ox, h=h: fwd(dz, ox, c, h).wait_send())


def body(n_slab, n_sub, blocks, prolong, columns, live, slots, coarse_of):
    rows, nbr = blocks.shape[:2]
    ncr = rows // 4
    n_x = n_sub // CORES
    half = n_x * ncr * CB
    hbm = pl.BlockSpec(memory_space=pltpu.HBM)
    dma = pltpu.SemaphoreType.DMA
    flops = 2 * rows * nbr * CB * BS * (BS + CB)
    return pl.pallas_call(
        functools.partial(kernel, n_slab, n_sub),
        out_shape=jax.ShapeDtypeStruct((ncr, CB, KC * CB), jnp.float32),
        in_specs=[hbm] * 6,
        out_specs=pl.BlockSpec(memory_space=pltpu.VMEM),
        scratch_shapes=[
            pltpu.SMEM((nbr, rows), jnp.int32), pltpu.SMEM((nbr, rows), jnp.int32),
            pltpu.SMEM((nbr, rows), jnp.int32), pltpu.SMEM((rows,), jnp.int32),
            pltpu.VMEM((3 * n_sub * rows, CB, BS), jnp.bfloat16),
            pltpu.VMEM((rows, nbr, BS, BS), jnp.bfloat16),
            pltpu.VMEM((rows, nbr * CB, 2 * BS), jnp.bfloat16),
            pltpu.VMEM((rows, nbr * CB, KC * CB), jnp.bfloat16),
            pltpu.VMEM((rows, 2 * CB, nbr * CB), jnp.bfloat16),
            pltpu.VMEM((CORES, rows * CB, KC * CB), jnp.bfloat16),
            pltpu.VMEM((CORES, 8, rows * CB), jnp.int32),
            pltpu.VMEM((3, half, CORES * rows * CB), jnp.bfloat16),
            pltpu.VMEM((3, half, KC * CB), jnp.float32),
            pltpu.VMEM((3, half, KC * CB), jnp.bfloat16),
            pltpu.VMEM((3, n_x, ncr * CB, KC * CB), jnp.bfloat16),
            dma((4,)), dma(()), dma((CHUNKS,)),
            dma((3, n_x, HALVES)), dma((3, n_x, HALVES)), dma((3, n_x, HALVES)), dma((3, n_x, HALVES)),
            dma(()), dma(()), dma((SHARES,)), dma((SHARES,)), dma((3, n_x)), dma((3, n_x)),
        ],
        compiler_params=pltpu.CompilerParams(
            collective_id=0, has_side_effects=True, vmem_limit_bytes=63 * 2 ** 20),
        cost_estimate=pl.CostEstimate(flops=flops, bytes_accessed=2 * blocks.size, transcendentals=0),
    )(columns.T, live.T, slots.T, coarse_of, prolong, blocks)


def solution(mesh):
    rows = ("groups", "slab", "sub")
    in_specs = (
        P(rows, None, None, None), P(rows, None, None),
        P(rows, None), P(rows, None), P(rows, None), P(rows),
    )
    part = functools.partial(body, mesh.shape["slab"], mesh.shape["sub"])
    return jax.shard_map(part, mesh=mesh, in_specs=in_specs, out_specs=P(rows, None, None), check_vma=False)
```

time: 26.9 us -> 23.5 us (0.87)
  Pallas kernels: 25.2 us -> 21.8 us
    pallas_call x1, Pallas kernels: 25.2 us -> 21.8 us  [body(): pl.pallas_call(functools.partial(kernel, n_slab, n_sub), out_shape=jax.Sh...]
where the time goes in v3:
time: 23.5 us; the launch traced here: 23.3 us
  Pallas kernels  21.8 us (93%)
  local copies, waits for them, and re-layouts  1.57 us (7%)
    pallas_call x1, Pallas kernels, body(): pl.pallas_call(functools.partial(kernel, n_slab, n_sub), out_shape=jax.Sh...  21.8 us
    unnamed x1, local copies, waits for them, and re-layouts  1.57 us

profile of v3, /device:TPU:0, one launch (start us, length us, event | category | flops | bytes accessed | tf_op | source)
XLA Modules:
  0.0 23.3 jit_solution(13413635590721291559)
XLA Ops:
  0.0 21.8 %shard_map.64 = f32[4,32,256]{2,1,0:T(8,128)} custom-call(s32[7,16]{1,0:T(8,128)} %bitcast.3, s32[7,16]{1,0:T(8,128)} %bitcast.4, s32[7,16]{1,0:T(8,128)} %bitcast.5, s32[16]{0:T(128)} %coarse_of_in.1, bf16[16,32,128]{2,1,0:T(8,128)(2,1)} %prolong.1, bf16[16,7,128,128]{3,2,1,0:T(8,128)(2,1)} %blocks.1), custom_call_target="tpu_custom_call" | custom-call | flops 146800640 | bytes 3670016 | tf_op jit(solution)/shard_map/pallas_call | solution.py:293
  21.8 1.6 %copy.8 = f32[4,32,256]{2,1,0:T(8,128)} copy(f32[4,32,256]{2,1,0:T(8,128)} %shard_map.64) | data formatting | bytes 262144

commit v4 on v3

--- a/solution.py
+++ b/solution.py
@@ -13,7 +13,7 @@
 CORES = 2
 CHUNKS = 4
 HALVES = 2
-DIRECT = 0
+ALONG_X = 1
 SHARES = 1
 MESH = pl.DeviceIdType.MESH
 NT = (((1,), (1,)), ((), ()))
@@ -88,13 +88,22 @@
     def spot(dz, ox, core, h):
         return wide.at[place(1 - dz, from_sub(ox, core), h)]
 
+    def last_x(dz, ox, h):
+        return dz != 0 and ox != 0 and h >= HALVES - ALONG_X
+
     def p1_send(dz, ox, h):
-        passed = dz != 0 and ox != 0 and h < HALVES - DIRECT
-        return pltpu.make_async_remote_copy(
-            src_ref=spot(0, ox, c, h) if passed else prolong.at[pl.ds(h * part, part)],
-            dst_ref=spot(dz, ox, c, h) if passed else wide.at[place(1 - dz, sub, h)],
+        dst = wide.at[place(1 - dz, sub, h)]
+        target = {"slab": z + dz, "sub": to_sub(ox)}
+        if dz == 0 or ox == 0:
+            src = prolong.at[pl.ds(h * part, part)]
+        elif last_x(dz, ox, h):
+            src, target = spot(dz, 0, c, h), {"slab": z, "sub": to_sub(ox)}
+        else:
+            src, dst, target = spot(0, ox, c, h), spot(dz, ox, c, h), {"slab": z + dz, "sub": sub}
+        return pltpu.make_async_remote_copy(
+            src_ref=src, dst_ref=dst,
             send_sem=p1s.at[dz + 1, ox, h], recv_sem=p1r.at[dz + 1, ox, h],
-            device_id={"slab": z + dz, "sub": sub if passed else to_sub(ox)}, device_id_type=MESH)
+            device_id=target, device_id_type=MESH)
 
     def p1_recv(dz, ox, h):
         return pltpu.make_async_remote_copy(
@@ -112,11 +121,7 @@
         for ox in range(1, n_x):
             p1_send(0, ox, h).start()
         for dz in (-1, 1):
-            there(dz, lambda dz=dz, h=h: p1_send(dz, 0, h).start())
-    for h in halves[HALVES - DIRECT:]:
-        for ox in range(1, n_x):
-            for dz in (-1, 1):
-                there(dz, lambda dz=dz, ox=ox, h=h: p1_send(dz, ox, h).start())
+            there(dz, lambda dz=dz, h=HALVES - 1 - h: p1_send(dz, 0, h).start())
     for h in halves:
         fwd(0, 0, c, h).start()
 
@@ -150,9 +155,12 @@
     def pass_on(dz, ox, h):
         def go():
             p1_recv(dz, ox, h).wait_recv()
-            if dz == 0 and h < HALVES - DIRECT:
+            if dz == 0 and h < HALVES - ALONG_X:
                 for to in (-1, 1):
                     there(to, lambda to=to: p1_send(to, ox, h).start())
+            if ox == 0 and h >= HALVES - ALONG_X:
+                for to in range(1, n_x):
+                    p1_send(dz, to, h).start()
             fwd(dz, ox, c, h).start()
         there(-dz, go)
 
@@ -165,10 +173,14 @@
 
     for n in range(CHUNKS // 2):
         rows_left(n)
-    for ox in range(1, n_x):
-        pass_on(0, ox, 0)
+    for h in halves[:HALVES - ALONG_X]:
+        for ox in range(1, n_x):
+            pass_on(0, ox, h)
+    for h in reversed(halves[HALVES - ALONG_X:]):
+        for dz in (-1, 1):
+            pass_on(dz, 0, h)
     rows_left(CHUNKS // 2)
-    for h in halves[1:]:
+    for h in halves[HALVES - ALONG_X:]:
         for ox in range(1, n_x):
             pass_on(0, ox, h)
     for n in range(CHUNKS // 2 + 1, CHUNKS):
@@ -183,7 +195,7 @@
             slot = jnp.where(live[k, i] != 0, slots[k, i], -1)
             sel[i, k * CB:(k + 1) * CB, :] = jnp.where(key == slot, 1.0, 0.0).astype(jnp.bfloat16)
 
-    for h in halves:
+    for h in reversed(halves[:HALVES - ALONG_X]):
         for dz in (-1, 1):
             pass_on(dz, 0, h)
 
@@ -199,7 +211,7 @@
                 picks[g, t * piece + q * CB:t * piece + (q + 1) * CB, :] = (
                     jnp.where(pick, 1.0, 0.0).astype(jnp.bfloat16))
 
-    for h in reversed(halves):
+    for h in halves:
         for ox in range(1, n_x):
             for dz in (-1, 1):
                 pass_on(dz, ox, h)
@@ -258,12 +270,15 @@
             device_id={"slab": z + dz, "sub": to_sub(ox)}, device_id_type=MESH)
 
     for g in groups:
-        sb[g] = (wo[g] + jnp.dot(picks[g, :, rows * CB:], tb[1], preferred_element_type=jnp.float32)).astype(jnp.bfloat16)
+        summed = wo[g] + jnp.dot(picks[g, :, rows * CB:], tb[1], preferred_element_type=jnp.float32)
+        sb[g] = summed.astype(jnp.bfloat16)
+        if g == 1:
+            wo[g] = summed
         for ox in reversed(range(n_x)):
             if (g - 1, ox) != (0, 0):
                 there(g - 1, lambda dz=g - 1, ox=ox: p2(dz, ox).start())
 
-    total = sb[1, pl.ds(pl.multiple_of(x * piece, piece), piece), :].astype(jnp.float32)
+    total = wo[1, pl.ds(pl.multiple_of(x * piece, piece), piece), :]
     for dz, ox in plane:
         there(-dz, lambda dz=dz, ox=ox: p2(dz, ox).wait_recv())
     for dz, ox in plane:
@@ -276,7 +291,8 @@
     for dz, ox in plane:
         there(dz, lambda dz=dz, ox=ox: p2(dz, ox).wait_send())
         for h in halves:
-            there(dz, lambda dz=dz, ox=ox, h=h: p1_send(dz, ox, h).wait_send())
+            there(-dz if last_x(dz, ox, h) else dz,
+                  lambda dz=dz, ox=ox, h=h: p1_send(dz, ox, h).wait_send())
     for dz, ox in offsets:
         for h in halves:
             there(-dz, lambda dz=dz, ox=ox, h=h: fwd(dz, ox, c, h).wait_send())

time: 23.5 us -> 23.5 us (level)
  no operation moved by 1% of the time
where the time goes in v4:
time: 23.5 us; the launch traced here: 23.3 us
  Pallas kernels  21.7 us (92%)
  local copies, waits for them, and re-layouts  1.57 us (7%)
    pallas_call x1, Pallas kernels, body(): pl.pallas_call(functools.partial(kernel, n_slab, n_sub), out_shape=jax.Sh...  21.7 us
    unnamed x1, local copies, waits for them, and re-layouts  1.57 us

profile of v4, /device:TPU:0, one launch (start us, length us, event | category | flops | bytes accessed | tf_op | source)
XLA Modules:
  0.0 23.3 jit_solution(12761181634499113479)
XLA Ops:
  0.0 21.7 %shard_map.64 = f32[4,32,256]{2,1,0:T(8,128)} custom-call(s32[7,16]{1,0:T(8,128)} %bitcast.3, s32[7,16]{1,0:T(8,128)} %bitcast.4, s32[7,16]{1,0:T(8,128)} %bitcast.5, s32[16]{0:T(128)} %coarse_of_in.1, bf16[16,32,128]{2,1,0:T(8,128)(2,1)} %prolong.1, bf16[16,7,128,128]{3,2,1,0:T(8,128)(2,1)} %blocks.1), custom_call_target="tpu_custom_call" | custom-call | flops 146800640 | bytes 3670016 | tf_op jit(solution)/shard_map/pallas_call | solution.py:309
  21.8 1.6 %copy.8 = f32[4,32,256]{2,1,0:T(8,128)} copy(f32[4,32,256]{2,1,0:T(8,128)} %shard_map.64) | data formatting | bytes 262144

commit v5 on v4

--- a/solution.py
+++ b/solution.py
@@ -81,9 +81,10 @@
 
     pl.semaphore_signal(barrier, inc=1, device_id={"sub": mate}, device_id_type=MESH)
     for dz, ox in plane:
-        there(dz, greet(dz, ox))
+        if dz == 0 or ox == 0:
+            there(dz, greet(dz, ox))
     ends = (z == 0).astype(jnp.int32) + (z == n_slab - 1).astype(jnp.int32)
-    pl.semaphore_wait(barrier, 3 * n_x - n_x * ends)
+    pl.semaphore_wait(barrier, n_x + 2 - ends)
 
     def spot(dz, ox, core, h):
         return wide.at[place(1 - dz, from_sub(ox, core), h)]

time: 23.5 us -> 23.3 us (level)
  no operation moved by 1% of the time
where the time goes in v5:
time: 23.3 us; the launch traced here: 23.1 us
  Pallas kernels  21.6 us (93%)
  local copies, waits for them, and re-layouts  1.57 us (7%)
    pallas_call x1, Pallas kernels, body(): pl.pallas_call(functools.partial(kernel, n_slab, n_sub), out_shape=jax.Sh...  21.6 us
    unnamed x1, local copies, waits for them, and re-layouts  1.57 us

profile of v5, /device:TPU:0, one launch (start us, length us, event | category | flops | bytes accessed | tf_op | source)
XLA Modules:
  0.0 23.1 jit_solution(6014083275098153945)
XLA Ops:
  0.0 21.6 %shard_map.64 = f32[4,32,256]{2,1,0:T(8,128)} custom-call(s32[7,16]{1,0:T(8,128)} %bitcast.3, s32[7,16]{1,0:T(8,128)} %bitcast.4, s32[7,16]{1,0:T(8,128)} %bitcast.5, s32[16]{0:T(128)} %coarse_of_in.1, bf16[16,32,128]{2,1,0:T(8,128)(2,1)} %prolong.1, bf16[16,7,128,128]{3,2,1,0:T(8,128)(2,1)} %blocks.1), custom_call_target="tpu_custom_call" | custom-call | flops 146800640 | bytes 3670016 | tf_op jit(solution)/shard_map/pallas_call | solution.py:310
  21.6 1.6 %copy.8 = f32[4,32,256]{2,1,0:T(8,128)} copy(f32[4,32,256]{2,1,0:T(8,128)} %shard_map.64) | data formatting | bytes 262144
